TPU v7x, 256 devices: a whole 4x4x8 slice. The times are simulated.
256 devices in a mesh: pair: 32 (over y_lo, z, core), freq: 8 (over x, y_hi).
Axes of the slice: x: 4, y: 4 (y_hi: 2, y_lo: 2; y = y_hi * 2 + y_lo), z: 8, core: 2. Of those that a mesh axis runs over, the one named last changes fastest.
Arguments:
- home_spectra: bfloat16 [8192, 2, 8, 512], P(('pair', 'freq')), may hold values from -6 to 6
- travel_spectra: bfloat16 [8192, 2, 8, 512], P(('pair', 'freq')), may hold values from -6 to 6
- rotation: int32 [1], replicated, may hold values from 0 to 31
Outputs:
- correlation: bfloat16 [1, 32, 256, 256, 128], P(None, 'pair', None, 'freq')
All inputs are finite; a program needn't handle non-finite values.
Results may differ from a plain program's by a relative error of at most 0.0058.
Values may be sent and summed in bfloat16 or wider, within the bound.
No kernel may reach another device: no remote copies, remote signals or barrier semaphores. Data moves between devices by JAX's collectives and lax.ppermute only.
A program may use at most 128 MiB of HBM per device.

v0:
```python
import math

import jax
import jax.numpy as jnp
from jax import lax
from jax.sharding import PartitionSpec as P

LAGS = 128


def passed_along(value, axis, by):
    count = lax.axis_size(axis)
    return lax.ppermute(value, axis, [(i, (i + by) % count) for i in range(count)])


def make_table(freq_count, lag_count, window_count):
    freq_index = jnp.arange(freq_count, dtype=jnp.int32)[:, None]
    lag_index = jnp.arange(lag_count, dtype=jnp.int32)[None, :] - lag_count // 2
    phase_step = freq_index * lag_index % (2 * freq_count)
    angles = phase_step.astype(jnp.float32) * (math.pi / freq_count)
    norm_scale = 1.0 / math.sqrt(2.0 * window_count * freq_count)
    return jnp.stack([jnp.cos(angles) * norm_scale, -jnp.sin(angles) * norm_scale], axis=0).astype(
        jnp.bfloat16
    )


def correlate(home_block, travel_block, lag_table):
    freq_count = home_block.shape[3]
    band_width = min(128, freq_count)
    turned = jnp.stack([-travel_block[:, 1], travel_block[:, 0]], axis=1)
    partner_terms = jnp.stack([travel_block, turned], axis=0)
    summed = jnp.zeros(
        (home_block.shape[0], travel_block.shape[0], lag_table.shape[2]), jnp.float32
    )
    for begin in range(0, freq_count, band_width):
        home_band = home_block[..., begin : begin + band_width]
        partner_band = partner_terms[..., begin : begin + band_width]
        cross = jnp.einsum(
            "hcwf,ptcwf->hptf", home_band, partner_band, preferred_element_type=jnp.float32
        ).astype(jnp.bfloat16)
        table_band = lag_table[:, begin : begin + band_width]
        summed = summed + jnp.einsum(
            "hptf,pfl->htl", cross, table_band, preferred_element_type=jnp.float32
        )
    return summed


def per_device(home_spectra, travel_spectra, rotation):
    window_count = home_spectra.shape[2]
    freq_count = home_spectra.shape[3]
    lag_table = make_table(freq_count, LAGS, window_count)
    pair_count = lax.axis_size("pair")
    offset = rotation[0]
    travel = travel_spectra
    for bit_index in range((pair_count - 1).bit_length()):
        shifted = passed_along(travel, "pair", 1 << bit_index)
        travel = jnp.where(offset >> bit_index & 1 == 1, shifted, travel)
    home_full = lax.all_gather(home_spectra, "freq", axis=0, tiled=True)
    summed = correlate(home_full, travel, lag_table)
    outputs = [summed.astype(jnp.bfloat16)]
    return jnp.stack(outputs, axis=0)[:, None]


def solution(mesh):
    in_specs = (P(("pair", "freq"), None, None, None), P(("pair", "freq"), None, None, None), P())
    out_specs = P(None, "pair", None, "freq", None)
    return jax.shard_map(
        per_device, mesh=mesh, in_specs=in_specs, out_specs=out_specs, check_vma=False
    )
```

profile of v0, /device:TPU:1, one launch (start us, length us, event | category | flops | bytes accessed | tf_op | source)
XLA Modules:
  0.0 213.6 jit_solution(10533751825849371775)
XLA Ops:
  6.5 0.0 all-gather.2.cloned.1.call-start
  6.5 0.7 all-gather.2.cloned.1.call-update
  7.3 3.1 %collective-permute-start = (bf16[32,2,8,512]{3,2,1,0:T(8,128)(2,1)}, bf16[32,2,8,512]{3,2,1,0:T(8,128)(2,1)S(1)}, u32[]{:S(2)}, u32[]{:S(2)}) collective-permute-start(bf16[32,2,8,512]{3,2,1,0:T(8,128)(2,1)} %param.4), channel_id=1, source_target_pairs={{0,8},{8,16},{16,24},{24,32},{32,40},{40,48},{48,56},{56,64},{64,7... | collective-permute-start | bytes 1572872 | tf_op jit(solution)/shard_map/ppermute | solution.py:13
  11.0 5.8 %collective-permute-done = bf16[32,2,8,512]{3,2,1,0:T(8,128)(2,1)S(1)} collective-permute-done((bf16[32,2,8,512]{3,2,1,0:T(8,128)(2,1)}, bf16[32,2,8,512]{3,2,1,0:T(8,128)(2,1)S(1)}, u32[]{:S(2)}, u32[]{:S(2)}) %collective-permute-start) | collective-permute-done | bytes 524320 | tf_op jit(solution)/shard_map/ppermute | solution.py:13
  16.8 1.1 broadcast_select_fusion
  17.9 1.7 collective-permute-start.1
  19.6 10.1 %collective-permute-done.1 = bf16[32,2,8,512]{3,2,1,0:T(8,128)(2,1)S(1)} collective-permute-done((bf16[32,2,8,512]{3,2,1,0:T(8,128)(2,1)S(1)}, bf16[32,2,8,512]{3,2,1,0:T(8,128)(2,1)S(1)}, u32[]{:S(2)}, u32[]{:S(2)}) %collective-permute-start.1) | collective-permute-done | bytes 524320 | tf_op jit(solution)/shard_map/ppermute | solution.py:13
  29.7 0.1 broadcast_select_fusion.1
  29.8 5.8 %collective-permute-start.2 = (bf16[32,2,8,512]{3,2,1,0:T(8,128)(2,1)S(1)}, bf16[32,2,8,512]{3,2,1,0:T(8,128)(2,1)S(1)}, u32[]{:S(2)}, u32[]{:S(2)}) collective-permute-start(bf16[32,2,8,512]{3,2,1,0:T(8,128)(2,1)S(1)} %broadcast_select_fusion.1), channel_id=1, source_target_pairs={{0,32},{8,40},{16,48},{24,56},{32,64},{40,72},{48,80},{56,88},{64,... | collective-permute-start | bytes 1572872 | tf_op jit(solution)/shard_map/ppermute | solution.py:13
  35.6 22.6 %collective-permute-done.2 = bf16[32,2,8,512]{3,2,1,0:T(8,128)(2,1)S(1)} collective-permute-done((bf16[32,2,8,512]{3,2,1,0:T(8,128)(2,1)S(1)}, bf16[32,2,8,512]{3,2,1,0:T(8,128)(2,1)S(1)}, u32[]{:S(2)}, u32[]{:S(2)}) %collective-permute-start.2) | collective-permute-done | bytes 524320 | tf_op jit(solution)/shard_map/ppermute | solution.py:13
  58.2 0.1 broadcast_select_fusion.2
  58.3 0.1 collective-permute-start.3
  58.4 17.9 %collective-permute-done.3 = bf16[32,2,8,512]{3,2,1,0:T(8,128)(2,1)S(1)} collective-permute-done((bf16[32,2,8,512]{3,2,1,0:T(8,128)(2,1)S(1)}, bf16[32,2,8,512]{3,2,1,0:T(8,128)(2,1)S(1)}, u32[]{:S(2)}, u32[]{:S(2)}) %collective-permute-start.3) | collective-permute-done | bytes 524320 | tf_op jit(solution)/shard_map/ppermute | solution.py:13
  76.2 0.1 broadcast_select_fusion.3
  76.3 0.5 collective-permute-start.4
  76.8 1.1 multiply_convert_fusion
  78.0 23.2 %collective-permute-done.4 = bf16[32,2,8,512]{3,2,1,0:T(8,128)(2,1)S(1)} collective-permute-done((bf16[32,2,8,512]{3,2,1,0:T(8,128)(2,1)S(1)}, bf16[32,2,8,512]{3,2,1,0:T(8,128)(2,1)S(1)}, u32[]{:S(2)}, u32[]{:S(2)}) %collective-permute-start.4) | collective-permute-done | bytes 524320 | tf_op jit(solution)/shard_map/ppermute | solution.py:13
  101.2 0.1 broadcast_select_fusion.4
  101.3 1.0 fusion.22
  102.3 1.5 copy.6
  103.8 1.5 copy.10
  105.3 2.7 %copy.18 = bf16[2,32,2,8,128]{1,3,2,0,4:T(8,128)(2,1)S(1)} copy(bf16[2,32,2,8,128]{4,3,2,1,0:T(8,128)(2,1)} %get-tuple-element.11) | data formatting | bytes 524288 | tf_op jit(solution)/shard_map/slice | solution.py:37
  108.0 3.6 %copy.14 = bf16[2,32,2,8,128]{1,3,2,0,4:T(8,128)(2,1)} copy(bf16[2,32,2,8,128]{4,3,2,1,0:T(8,128)(2,1)} %get-tuple-element.12) | data formatting | bytes 524288 | tf_op jit(solution)/shard_map/slice | solution.py:37
  111.7 11.3 %all-gather.2.cloned.1.call-done = bf16[256,2,8,512]{3,2,1,0:T(8,128)(2,1)} async-done(((bf16[32,2,8,512]{3,2,1,0:T(8,128)(2,1)}), bf16[256,2,8,512]{3,2,1,0:T(8,128)(2,1)}) %all-gather.2.cloned.1.call-update) | async-done | bytes 4194320 | tf_op jit(solution)/shard_map/all_gather | solution.py:58
  123.0 4.6 %slice_bitcast_fusion.3 = (bf16[256,2,8,128,1]{3,2,1,0,4:T(8,128)(2,1)}, bf16[256,2,8,128,1]{3,2,1,0,4:T(8,128)(2,1)}, bf16[256,2,8,128,1]{3,2,1,0,4:T(8,128)(2,1)}, bf16[256,2,8,128,1]{3,2,1,0,4:T(8,128)(2,1)}) fusion(bf16[256,2,8,512]{3,2,1,0:T(8,128)(2,1)} %all-gather.2.cloned.1.call-done), kind=kLoop, calls=%fused_computation.26 | loop fusion | bytes 8388608 | tf_op jit(solution)/shard_map/slice | solution.py:36
  127.6 3.0 %copy.7 = bf16[256,2,8,128,1]{0,2,1,4,3:T(8,128)(2,1)} copy(bf16[256,2,8,128,1]{3,2,1,0,4:T(8,128)(2,1)} %get-tuple-element.5) | data formatting | bytes 2097152 | tf_op jit(solution)/shard_map/slice | solution.py:36
  130.6 3.0 %copy.19 = bf16[256,2,8,128,1]{0,2,1,4,3:T(8,128)(2,1)} copy(bf16[256,2,8,128,1]{3,2,1,0,4:T(8,128)(2,1)} %get-tuple-element.6) | data formatting | bytes 2097152 | tf_op jit(solution)/shard_map/slice | solution.py:36
  133.6 3.0 %copy.15 = bf16[256,2,8,128,1]{0,2,1,4,3:T(8,128)(2,1)} copy(bf16[256,2,8,128,1]{3,2,1,0,4:T(8,128)(2,1)} %get-tuple-element.7) | data formatting | bytes 2097152 | tf_op jit(solution)/shard_map/slice | solution.py:36
  136.6 3.0 %copy.11 = bf16[256,2,8,128,1]{0,2,1,4,3:T(8,128)(2,1)} copy(bf16[256,2,8,128,1]{3,2,1,0,4:T(8,128)(2,1)} %get-tuple-element.8) | data formatting | bytes 2097152 | tf_op jit(solution)/shard_map/slice | solution.py:36
  139.6 4.5 %fusion.44 = bf16[128,2,32,256,1]{3,2,4,1,0:T(8,128)(2,1)} fusion(bf16[2,32,2,8,128]{1,3,2,0,4:T(8,128)(2,1)S(1)} %copy.10, bf16[256,2,8,128,1]{0,2,1,4,3:T(8,128)(2,1)} %copy.11), kind=kOutput, calls=%fused_computation.70 | convolution fusion | flops 67108864 | bytes 5505024 | tf_op jit(solution)/shard_map/hcwf,ptcwf->hptf/dot_general | solution.py:38
  144.1 8.0 %copy.12 = bf16[128,2,32,256,1]{0,3,1,2,4:T(8,128)(2,1)} copy(bf16[128,2,32,256,1]{3,2,4,1,0:T(8,128)(2,1)} %fusion.44) | data formatting | bytes 8388608 | tf_op jit(solution)/shard_map/hcwf,ptcwf->hptf/dot_general | solution.py:38
  152.1 0.0 copy-done.3
  152.1 4.5 %fusion.45 = bf16[128,2,32,256,1]{3,2,4,1,0:T(8,128)(2,1)} fusion(bf16[2,32,2,8,128]{1,3,2,0,4:T(8,128)(2,1)S(1)} %copy-done.3, bf16[256,2,8,128,1]{0,2,1,4,3:T(8,128)(2,1)} %copy.15), kind=kOutput, calls=%fused_computation.71 | convolution fusion | flops 67108864 | bytes 5505024 | tf_op jit(solution)/shard_map/hcwf,ptcwf->hptf/dot_general | solution.py:38
  156.6 7.9 %copy.16 = bf16[128,2,32,256,1]{0,3,1,2,4:T(8,128)(2,1)} copy(bf16[128,2,32,256,1]{3,2,4,1,0:T(8,128)(2,1)} %fusion.45) | data formatting | bytes 8388608 | tf_op jit(solution)/shard_map/hcwf,ptcwf->hptf/dot_general | solution.py:38
  164.5 5.5 %fusion.4 = f32[256,32,128,1]{2,0,3,1:T(8,128)} fusion(bf16[128,2,32,256,1]{0,3,1,2,4:T(8,128)(2,1)} %copy.12, bf16[1,512,128]{2,1,0:T(8,128)(2,1)S(1)} %get-tuple-element.16, bf16[1,512,128]{2,1,0:T(8,128)(2,1)S(1)} %get-tuple-element.15), kind=kOutput, calls=%fused_computation.7 | convolution fusion | flops 536903680 | bytes 8650752 | tf_op jit(solution)/shard_map/hptf,pfl->htl/dot_general | solution.py:42
  170.1 0.0 copy-done
  170.1 3.2 %fusion.7 = f32[256,32,128,1]{2,0,3,1:T(8,128)} fusion(bf16[128,2,32,256,1]{0,3,1,2,4:T(8,128)(2,1)S(1)} %copy-done, bf16[1,512,128]{2,1,0:T(8,128)(2,1)S(1)} %get-tuple-element.16, bf16[1,512,128]{2,1,0:T(8,128)(2,1)S(1)} %get-tuple-element.15), kind=kOutput, calls=%fused_computation.9 | convolution fusion | flops 536903680 | bytes 8650752 | tf_op jit(solution)/shard_map/hptf,pfl->htl/dot_general | solution.py:42
  173.3 0.0 copy-done.5
  173.3 3.2 %fusion.46 = bf16[128,2,32,256,1]{3,2,4,1,0:T(8,128)(2,1)} fusion(bf16[2,32,2,8,128]{1,3,2,0,4:T(8,128)(2,1)S(1)} %copy.18, bf16[256,2,8,128,1]{0,2,1,4,3:T(8,128)(2,1)S(1)} %copy-done.5), kind=kOutput, calls=%fused_computation.72 | convolution fusion | flops 67108864 | bytes 5505024 | tf_op jit(solution)/shard_map/hcwf,ptcwf->hptf/dot_general | solution.py:38
  176.5 8.0 %copy.20 = bf16[128,2,32,256,1]{0,3,1,2,4:T(8,128)(2,1)} copy(bf16[128,2,32,256,1]{3,2,4,1,0:T(8,128)(2,1)} %fusion.46) | data formatting | bytes 8388608 | tf_op jit(solution)/shard_map/hcwf,ptcwf->hptf/dot_general | solution.py:38
  184.5 0.0 copy-done.4
  184.5 3.2 %fusion.43 = bf16[128,2,32,256,1]{3,2,4,1,0:T(8,128)(2,1)} fusion(bf16[2,32,2,8,128]{1,3,2,0,4:T(8,128)(2,1)S(1)} %copy.6, bf16[256,2,8,128,1]{0,2,1,4,3:T(8,128)(2,1)S(1)} %copy-done.4), kind=kOutput, calls=%fused_computation.69 | convolution fusion | flops 67108864 | bytes 5505024 | tf_op jit(solution)/shard_map/hcwf,ptcwf->hptf/dot_general | solution.py:38
  187.8 7.9 %copy.8 = bf16[128,2,32,256,1]{0,3,1,2,4:T(8,128)(2,1)} copy(bf16[128,2,32,256,1]{3,2,4,1,0:T(8,128)(2,1)} %fusion.43) | data formatting | bytes 8388608 | tf_op jit(solution)/shard_map/hcwf,ptcwf->hptf/dot_general | solution.py:38
  195.7 3.6 %fusion.1 = f32[256,32,128,1]{2,0,3,1:T(8,128)S(1)} fusion(bf16[128,2,32,256,1]{0,3,1,2,4:T(8,128)(2,1)} %copy.8, bf16[1,512,128]{2,1,0:T(8,128)(2,1)S(1)} %get-tuple-element.16, bf16[1,512,128]{2,1,0:T(8,128)(2,1)S(1)} %get-tuple-element.15), kind=kOutput, calls=%fused_computation.5 | convolution fusion | flops 536903680 | bytes 8650752 | tf_op jit(solution)/shard_map/hptf,pfl->htl/dot_general | solution.py:42
  199.3 0.0 copy-done.1
  199.3 1.1 copy-done.2
  200.4 3.6 %fusion.15 = bf16[1,1,256,32,128]{4,2,3,1,0:T(8,128)(2,1)S(1)} fusion(bf16[128,2,32,256,1]{0,3,1,2,4:T(8,128)(2,1)} %copy.20, f32[256,32,128,1]{2,0,3,1:T(8,128)S(1)} %copy-done.2, f32[256,32,128,1]{2,0,3,1:T(8,128)S(1)} %copy-done.1, f32[256,32,128,1]{2,0,3,1:T(8,128)S(1)} %fusion.1, bf16[1,512,128]{2,1,0:T(8,128)(2,1)S(1)} %get-tuple-element.15, ...), kind=kOutput, calls=%fused_computation.16 | convolution fusion | flops 541196288 | bytes 19136512 | tf_op jit(solution)/shard_map/hptf,pfl->htl/dot_general | solution.py:42
  204.0 2.7 %copy.5 = bf16[1,1,256,32,128]{4,3,2,1,0:T(8,128)(2,1)} copy(bf16[1,1,256,32,128]{4,2,3,1,0:T(8,128)(2,1)S(1)} %fusion.15) | data formatting | bytes 4194304 | tf_op jit(solution)/shard_map/broadcast_in_dim;stack | solution.py:61
  (9 shorter events, 0.1 us)
Async XLA Ops:
  6.5 116.5 %all-gather.2.cloned.1.call-start = ((), (), s32[]{:S(2)}) async-start(), calls=%async_computation | async-start | bytes 4718592 | tf_op jit(solution)/shard_map/all_gather | solution.py:58
  7.3 9.5 %collective-permute-start = (bf16[32,2,8,512]{3,2,1,0:T(8,128)(2,1)}, bf16[32,2,8,512]{3,2,1,0:T(8,128)(2,1)S(1)}, u32[]{:S(2)}, u32[]{:S(2)}) collective-permute-start(bf16[32,2,8,512]{3,2,1,0:T(8,128)(2,1)} %param.4), channel_id=1, source_target_pairs={{0,8},{8,16},{16,24},{24,32},{32,40},{40,48},{48,56},{56,64},{64,7... | collective-permute-start | bytes 1572872 | tf_op jit(solution)/shard_map/ppermute | solution.py:13
  17.9 11.8 %collective-permute-start.1 = (bf16[32,2,8,512]{3,2,1,0:T(8,128)(2,1)S(1)}, bf16[32,2,8,512]{3,2,1,0:T(8,128)(2,1)S(1)}, u32[]{:S(2)}, u32[]{:S(2)}) collective-permute-start(bf16[32,2,8,512]{3,2,1,0:T(8,128)(2,1)S(1)} %broadcast_select_fusion), channel_id=1, source_target_pairs={{0,16},{8,24},{16,32},{24,40},{32,48},{40,56},{48,64},{56,72},{64,... | collective-permute-start | bytes 1572872 | tf_op jit(solution)/shard_map/ppermute | solution.py:13
  29.8 28.4 %collective-permute-start.2 = (bf16[32,2,8,512]{3,2,1,0:T(8,128)(2,1)S(1)}, bf16[32,2,8,512]{3,2,1,0:T(8,128)(2,1)S(1)}, u32[]{:S(2)}, u32[]{:S(2)}) collective-permute-start(bf16[32,2,8,512]{3,2,1,0:T(8,128)(2,1)S(1)} %broadcast_select_fusion.1), channel_id=1, source_target_pairs={{0,32},{8,40},{16,48},{24,56},{32,64},{40,72},{48,80},{56,88},{64,... | collective-permute-start | bytes 1572872 | tf_op jit(solution)/shard_map/ppermute | solution.py:13
  58.3 18.0 %collective-permute-start.3 = (bf16[32,2,8,512]{3,2,1,0:T(8,128)(2,1)S(1)}, bf16[32,2,8,512]{3,2,1,0:T(8,128)(2,1)S(1)}, u32[]{:S(2)}, u32[]{:S(2)}) collective-permute-start(bf16[32,2,8,512]{3,2,1,0:T(8,128)(2,1)S(1)} %broadcast_select_fusion.2), channel_id=1, source_target_pairs={{0,64},{8,72},{16,80},{24,88},{32,96},{40,104},{48,112},{56,120},{... | collective-permute-start | bytes 1572872 | tf_op jit(solution)/shard_map/ppermute | solution.py:13
  76.3 24.9 %collective-permute-start.4 = (bf16[32,2,8,512]{3,2,1,0:T(8,128)(2,1)S(1)}, bf16[32,2,8,512]{3,2,1,0:T(8,128)(2,1)S(1)}, u32[]{:S(2)}, u32[]{:S(2)}) collective-permute-start(bf16[32,2,8,512]{3,2,1,0:T(8,128)(2,1)S(1)} %broadcast_select_fusion.3), channel_id=1, source_target_pairs={{0,128},{8,136},{16,144},{24,152},{32,160},{40,168},{48,176},{56,1... | collective-permute-start | bytes 1572872 | tf_op jit(solution)/shard_map/ppermute | solution.py:13
  144.1 8.0 %copy-start.3 = (bf16[2,32,2,8,128]{1,3,2,0,4:T(8,128)(2,1)S(1)}, bf16[2,32,2,8,128]{1,3,2,0,4:T(8,128)(2,1)}, u32[]{:S(2)}) copy-start(bf16[2,32,2,8,128]{1,3,2,0,4:T(8,128)(2,1)} %copy.14) | copy-start | bytes 786436
  164.5 5.6 %copy-start = (bf16[128,2,32,256,1]{0,3,1,2,4:T(8,128)(2,1)S(1)}, bf16[128,2,32,256,1]{0,3,1,2,4:T(8,128)(2,1)}, u32[]{:S(2)}) copy-start(bf16[128,2,32,256,1]{0,3,1,2,4:T(8,128)(2,1)} %copy.16) | copy-start | bytes 12582916
  170.1 3.2 %copy-start.5 = (bf16[256,2,8,128,1]{0,2,1,4,3:T(8,128)(2,1)S(1)}, bf16[256,2,8,128,1]{0,2,1,4,3:T(8,128)(2,1)}, u32[]{:S(2)}) copy-start(bf16[256,2,8,128,1]{0,2,1,4,3:T(8,128)(2,1)} %copy.19) | copy-start | bytes 3145732
  176.5 8.0 %copy-start.4 = (bf16[256,2,8,128,1]{0,2,1,4,3:T(8,128)(2,1)S(1)}, bf16[256,2,8,128,1]{0,2,1,4,3:T(8,128)(2,1)}, u32[]{:S(2)}) copy-start(bf16[256,2,8,128,1]{0,2,1,4,3:T(8,128)(2,1)} %copy.7) | copy-start | bytes 3145732
  195.7 3.6 %copy-start.1 = (f32[256,32,128,1]{2,0,3,1:T(8,128)S(1)}, f32[256,32,128,1]{2,0,3,1:T(8,128)}, u32[]{:S(2)}) copy-start(f32[256,32,128,1]{2,0,3,1:T(8,128)} %fusion.4) | copy-start | bytes 12582916
  195.7 4.7 %copy-start.2 = (f32[256,32,128,1]{2,0,3,1:T(8,128)S(1)}, f32[256,32,128,1]{2,0,3,1:T(8,128)}, u32[]{:S(2)}) copy-start(f32[256,32,128,1]{2,0,3,1:T(8,128)} %fusion.7) | copy-start | bytes 12582916
Sparse Core Ops, SparseCore 0:
  10.0 112.9 all-gather.1
where the time goes:
time: 214 us
  waiting for transfers between devices  91.7 us (43%)
  local copies, waits for them, and re-layouts  61.6 us (29%)
  matrix products  31.4 us (15%)
  between operations  14.2 us (7%)
  starting transfers between devices  11.2 us (5%)
  other arithmetic  3.51 us (2%)
    ppermute x5, waiting for transfers between devices, passed_along(): lax.ppermute(value, axis, [(i, (i + by) % count) for i in range(count)])  79.6 us
    dot_general x4, local copies, waits for them, and re-layouts, correlate(): jnp.einsum('hcwf,ptcwf->hptf', home_band, partner_band, preferred_element...  31.9 us
    slice x5, local copies, waits for them, and re-layouts, correlate(): home_band = home_block[..., begin:begin + band_width]  16.6 us
    dot_general x4, matrix products, correlate(): jnp.einsum('hptf,pfl->htl', cross, table_band, preferred_element_type=jnp...  16 us
    dot_general x4, matrix products, correlate(): jnp.einsum('hcwf,ptcwf->hptf', home_band, partner_band, preferred_element...  15.4 us
    all_gather x1, waiting for transfers between devices, per_device(): home_full = lax.all_gather(home_spectra, 'freq', axis=0, tiled=True)  11.3 us
    ppermute x5, starting transfers between devices, passed_along(): lax.ppermute(value, axis, [(i, (i + by) % count) for i in range(count)])  11.2 us
    slice x4, local copies, waits for them, and re-layouts, correlate(): partner_band = partner_terms[..., begin:begin + band_width]  9.3 us
  transfers between devices with their start and end apart: 6, of which 6 were waited for; matrix products, arithmetic and copies ran while one was open for 6% of the time, Pallas kernels for 0%

commit v1 on v0

v1 whole, which is shorter than its diff:
```python
import functools
import math

import jax
import jax.numpy as jnp
from jax import lax
from jax.experimental import pallas as pl
from jax.experimental.pallas import tpu as pltpu
from jax.sharding import PartitionSpec as P

LAGS = 128
BAND = 128
RUN = 8


def make_table(freq_count, lag_count, window_count):
    freq_index = jnp.arange(freq_count, dtype=jnp.int32)[None, :]
    lag_index = jnp.arange(lag_count, dtype=jnp.int32)[:, None] - lag_count // 2
    phase_step = freq_index * lag_index % (2 * freq_count)
    angles = phase_step.astype(jnp.float32) * (math.pi / freq_count)
    norm_scale = 1.0 / math.sqrt(2.0 * window_count * freq_count)
    table = [jnp.cos(angles) * norm_scale, -jnp.sin(angles) * norm_scale]
    return jnp.concatenate(table, axis=1).astype(jnp.bfloat16)


def along(value, axis, by):
    count = lax.axis_size(axis)
    return lax.ppermute(value, axis, [(i, (i + by) % count) for i in range(count)])


def ring(value, step):
    return along(value, "freq", 2 * step)


def across(value):
    return lax.ppermute(value, "freq", [(i, i ^ 1) for i in range(lax.axis_size("freq"))])


def places_of(side):
    me = lax.axis_index("freq")
    place, row = me // 2, me % 2
    found = [((place + step) % 4) * 2 + (row ^ side) for step in (0, -1, 1, 2)]
    return jnp.stack(found).astype(jnp.int32)


def moved(value, index, choices, unit):
    def branch(by):
        return lambda v: along(v, "pair", by * unit) if by else v

    return lax.switch(index, [branch(by) for by in choices], value)


def kernel(places, *refs, piece_count, first):
    pieces, travel, table = refs[:piece_count], refs[piece_count], refs[piece_count + 1]
    if first:
        out, terms, wide, weights, cross, turned, ready, sems = refs[piece_count + 2 :]
    else:
        terms = travel
        out, wide, weights, cross, turned, ready, sems = refs[piece_count + 3 :]
    _, term_count, band = pieces[0].shape
    channels, _, _, home_count = cross.shape
    half = term_count // 2
    groups = band // RUN
    lanes = term_count * RUN
    step = pl.program_id(0)

    begin = 0
    for piece in pieces:
        rows = piece.shape[0] * term_count
        wide[begin : begin + rows] = piece[...].astype(jnp.float32).reshape(rows, band)
        begin += rows

    def of_term(k):
        rows = wide[pl.ds(k, home_count, stride=term_count), :]
        return rows.astype(jnp.bfloat16).T.astype(jnp.float32).reshape(groups, RUN, home_count)

    for k in range(0, term_count, 2):
        two = jnp.concatenate([of_term(k), of_term(k + 1)], axis=1).astype(jnp.bfloat16)
        weights[:, k * RUN : (k + 2) * RUN, :home_count] = two
        if k < half:
            weights[:, (k + half) * RUN : (k + half + 2) * RUN, home_count:] = -two
        else:
            weights[:, (k - half) * RUN : (k - half + 2) * RUN, home_count:] = two

    if first:
        many = lanes // term_count
        blocks = channels // many
        sides = [travel[c : c + many].reshape(lanes, band).T for c in range(0, channels, many)]
        side = jnp.concatenate(sides, axis=0)
        spread_row = lax.broadcasted_iota(jnp.int32, (lanes, 2 * lanes), 0)
        spread_lane = lax.broadcasted_iota(jnp.int32, (lanes, 2 * lanes), 1)
        row = lax.broadcasted_iota(jnp.int32, (2 * RUN, lanes), 0)
        lane = lax.broadcasted_iota(jnp.int32, (2 * RUN, lanes), 1)
        diagonal = jnp.where(row % RUN == lane % RUN, 1.0, 0.0).astype(jnp.bfloat16)
        for j in range(many // 2):
            chosen = spread_row == 2 * j * term_count + spread_lane // RUN
            spread = jnp.where(chosen, 1.0, 0.0).astype(jnp.bfloat16)
            found = jnp.dot(side, spread, preferred_element_type=jnp.float32)
            found = found.reshape(blocks, groups, RUN, 2 * lanes)
            found = jnp.concatenate([found[..., :lanes], found[..., lanes:]], axis=2)
            found = found.astype(jnp.bfloat16) * diagonal
            for c in range(blocks):
                at = (c * many + 2 * j) * RUN
                terms[:, at : at + 2 * RUN, :] = found[c]

    for g in range(0, groups, 2):
        two = [
            jnp.dot(terms[g + i], weights[g + i], preferred_element_type=jnp.float32)
            for i in range(2)
        ]
        two = [x.reshape(channels, RUN, 2 * home_count) for x in two]
        found = jnp.concatenate(two, axis=1).astype(jnp.bfloat16)
        to = pl.ds(pl.multiple_of(step * band + g * RUN, 2 * RUN), 2 * RUN)
        cross[:, 0, to, :] = found[..., :home_count]
        cross[:, 1, to, :] = found[..., home_count:]

    @pl.when(step == pl.num_programs(0) - 1)
    def _():
        for t in range(0, channels, 2):
            two = [cross[t + i].reshape(-1, home_count) for i in range(2)]
            product = jnp.dot(
                table[...], jnp.concatenate(two, axis=1), preferred_element_type=jnp.float32
            )
            turned[t * home_count : (t + 2) * home_count] = (
                product.astype(jnp.bfloat16).T.astype(jnp.float32)
            )
        block = home_count // piece_count
        copies = []
        for b in range(piece_count):
            for i in range(b * block, (b + 1) * block):
                rows = turned[pl.ds(i, channels, stride=home_count), :]
                ready[i] = rows.astype(jnp.bfloat16)
            to = pl.ds(pl.multiple_of(places[b] * block, block), block)
            copies.append(
                pltpu.make_async_copy(ready.at[pl.ds(b * block, block)], out.at[to], sems.at[b])
            )
            copies[-1].start()
        for copy in copies:
            copy.wait()


def correlate(pieces, travel, table, places, home_total, so_far=None):
    first = so_far is None
    _, term_count, freq_count = pieces[0].shape
    home_count = sum(piece.shape[0] for piece in pieces)
    lag_count = table.shape[0]
    channels = travel.shape[0] if first else travel.shape[1] // RUN
    lanes = term_count * RUN
    spec = lambda n: pl.BlockSpec((n, term_count, BAND), lambda c: (0, 0, c))
    term_spec = pl.BlockSpec((BAND // RUN, channels * RUN, lanes), lambda c: (c, 0, 0))
    term_shape = jax.ShapeDtypeStruct((freq_count // RUN, channels * RUN, lanes), jnp.bfloat16)
    out_spec = pl.BlockSpec(memory_space=pl.ANY)
    out_shape = jax.ShapeDtypeStruct((home_total, channels, lag_count), jnp.bfloat16)
    earlier = [] if first else [so_far]
    return pl.pallas_call(
        functools.partial(kernel, piece_count=len(pieces), first=first),
        grid=(freq_count // BAND,),
        in_specs=[pl.BlockSpec(memory_space=pltpu.SMEM)]
        + [spec(piece.shape[0]) for piece in pieces]
        + [spec(channels) if first else term_spec]
        + [pl.BlockSpec((lag_count, 2 * freq_count), lambda c: (0, 0))]
        + [out_spec] * len(earlier),
        out_specs=[out_spec, term_spec] if first else out_spec,
        out_shape=[out_shape, term_shape] if first else out_shape,
        scratch_shapes=[
            pltpu.VMEM((home_count * term_count, BAND), jnp.float32),
            pltpu.VMEM((BAND // RUN, lanes, 2 * home_count), jnp.bfloat16),
            pltpu.VMEM((channels, 2, freq_count, home_count), jnp.bfloat16),
            pltpu.VMEM((home_count * channels, lag_count), jnp.float32),
            pltpu.VMEM((home_count, channels, lag_count), jnp.bfloat16),
            pltpu.SemaphoreType.DMA((len(pieces),)),
        ],
        input_output_aliases={} if first else {len(pieces) + 3: 0},
        compiler_params=pltpu.CompilerParams(vmem_limit_bytes=32 * 2**20),
        cost_estimate=pl.CostEstimate(
            flops=2 * channels * home_count * freq_count * (32 * term_count + 2 * lag_count),
            bytes_accessed=8 * 2**20,
            transcendentals=0,
        ),
    )(places, *pieces, travel, table, *earlier)


def per_device(home_spectra, travel_spectra, rotation):
    own_count, parts, window_count, freq_count = home_spectra.shape
    home_total = own_count * lax.axis_size("freq")
    own = home_spectra.reshape(own_count, parts * window_count, freq_count)
    travel = travel_spectra.reshape(own_count, parts * window_count, freq_count)
    table = make_table(freq_count, LAGS, window_count)

    far = ring(own, 2)
    left = ring(own, 1)
    right = ring(own, -1)
    other = across(own)
    fine = rotation[0] & 3
    coarse = ((rotation[0] + 1) >> 2) & 7
    travel = moved(travel, fine, (0, 1, 2, -1), 1)
    travel = moved(travel, coarse, (0, 1, 2, 3, 4, 5, 6, 7), 4)
    far, left, right, other, travel = lax.optimization_barrier((far, left, right, other, travel))

    other_left = ring(other, 1)
    other_right = ring(other, -1)
    other_far = across(far)
    row = [own, left, right, far]
    found, terms = correlate(row, travel, table, places_of(0), home_total)
    others = [other, other_left, other_right, other_far]
    found = correlate(others, terms, table, places_of(1), home_total, found)
    return found[None, None]


def solution(mesh):
    in_specs = (P(("pair", "freq"), None, None, None), P(("pair", "freq"), None, None, None), P())
    out_specs = P(None, "pair", None, "freq", None)
    return jax.shard_map(
        per_device, mesh=mesh, in_specs=in_specs, out_specs=out_specs, check_vma=False
    )
```

time: 214 us -> 77.1 us (0.36)
  the two profiles are of different devices: /device:TPU:1 before, /device:TPU:41 now
where the time goes in v1:
time: 77.1 us; the launch traced here: 75.8 us
  waiting for transfers between devices  36.4 us (47%)
  Pallas kernels  19.6 us (25%)
  starting transfers between devices  16.3 us (21%)
  other arithmetic  1.41 us (2%)
  local copies, waits for them, and re-layouts  1.12 us (1%)
  between operations  0.92 us (1%)
    ppermute x7, waiting for transfers between devices, along(): lax.ppermute(value, axis, [(i, (i + by) % count) for i in range(count)])  33 us
    pallas_call x2, Pallas kernels, correlate(): pl.pallas_call(functools.partial(kernel, piece_count=len(pieces), first=f...  19.6 us
    ppermute x7, starting transfers between devices, along(): lax.ppermute(value, axis, [(i, (i + by) % count) for i in range(count)])  14.3 us
    ppermute x2, waiting for transfers between devices, across(): lax.ppermute(value, 'freq', [(i, i ^ 1) for i in range(lax.axis_size('fre...  3.39 us
    ppermute x2, starting transfers between devices, across(): lax.ppermute(value, 'freq', [(i, i ^ 1) for i in range(lax.axis_size('fre...  2.02 us
  transfers between devices with their start and end apart: 9, of which 4 were waited for; matrix products, arithmetic and copies ran while one was open for 2% of the time, Pallas kernels for 13%

profile of v1, /device:TPU:41, one launch (start us, length us, event | category | flops | bytes accessed | tf_op | source)
XLA Modules:
  0.0 75.8 jit_solution(13282714685088133067)
XLA Ops:
  0.0 1.0 %copy.20 = bf16[32,2,8,512]{3,2,1,0:T(8,128)(2,1)S(1)} copy(bf16[32,2,8,512]{3,2,1,0:T(8,128)(2,1)} %param.16) | data formatting | bytes 1048576
  1.0 2.7 %collective-permute-start.10 = (bf16[32,16,512]{2,1,0:T(8,128)(2,1)}, bf16[32,16,512]{2,1,0:T(8,128)(2,1)S(1)}, u32[]{:S(2)}, u32[]{:S(2)}) collective-permute-start(bf16[32,16,512]{2,1,0:T(8,128)(2,1)} %bitcast.13), channel_id=1, source_target_pairs={{0,4},{1,5},{2,6},{3,7},{4,0},{5,1},{6,2},{7,3},{8,12},{9,13},{10,... | collective-permute-start | bytes 1572872 | tf_op jit(solution)/shard_map/ppermute | solution.py:28
  3.8 0.3 collective-permute-start.11
  4.1 2.4 %collective-permute-start.12 = (bf16[32,16,512]{2,1,0:T(8,128)(2,1)}, bf16[32,16,512]{2,1,0:T(8,128)(2,1)S(1)}, u32[]{:S(2)}, u32[]{:S(2)}) collective-permute-start(bf16[32,16,512]{2,1,0:T(8,128)(2,1)} %bitcast.15), channel_id=1, source_target_pairs={{0,6},{1,7},{2,0},{3,1},{4,2},{5,3},{6,4},{7,5},{8,14},{9,15},{10,... | collective-permute-start | bytes 1572872 | tf_op jit(solution)/shard_map/ppermute | solution.py:28
  6.5 2.0 %collective-permute-start.13 = (bf16[32,16,512]{2,1,0:T(8,128)(2,1)}, bf16[32,16,512]{2,1,0:T(8,128)(2,1)S(1)}, u32[]{:S(2)}, u32[]{:S(2)}) collective-permute-start(bf16[32,16,512]{2,1,0:T(8,128)(2,1)} %bitcast.16), channel_id=1, source_target_pairs={{0,1},{1,0},{2,3},{3,2},{4,5},{5,4},{6,7},{7,6},{8,9},{9,8},{10,11... | collective-permute-start | bytes 1572872 | tf_op jit(solution)/shard_map/ppermute | solution.py:36
  9.1 10.6 %conditional.2 = (bf16[32,16,512]{2,1,0:T(8,128)(2,1)S(1)}) conditional(s32[]{:T(128)} %bitcast.6, bf16[32,16,512]{2,1,0:T(8,128)(2,1)S(1)} %bitcast.18, bf16[32,16,512]{2,1,0:T(8,128)(2,1)S(1)} %bitcast.19, bf16[32,16,512]{2,1,0:T(8,128)(2,1)S(1)} %bitcast.20, bf16[32,16,512]{2,1,0:T(8,128)(2,1)S(1)} %bitcast.21), branch_computations={%region_0.1_spmd, %region_1.2_spmd, %region_2.3_spmd, %region_3.4_... | conditional | bytes 3145776 | solution.py:50
  9.2 1.9 %collective-permute-start.2 = (bf16[32,16,512]{2,1,0:T(8,128)(2,1)S(1)}, bf16[32,16,512]{2,1,0:T(8,128)(2,1)S(1)}, u32[]{:S(2)}, u32[]{:S(2)}) collective-permute-start(bf16[32,16,512]{2,1,0:T(8,128)(2,1)S(1)} %param.3), channel_id=1, source_target_pairs={{0,248},{8,0},{16,8},{24,16},{32,24},{40,32},{48,40},{56,48},{64,5... | collective-permute-start | bytes 1572872 | tf_op jit(solution)/shard_map/cond/branch_3_fun/ppermute | solution.py:28
  11.0 8.7 %collective-permute-done.2 = bf16[32,16,512]{2,1,0:T(8,128)(2,1)S(1)} collective-permute-done((bf16[32,16,512]{2,1,0:T(8,128)(2,1)S(1)}, bf16[32,16,512]{2,1,0:T(8,128)(2,1)S(1)}, u32[]{:S(2)}, u32[]{:S(2)}) %collective-permute-start.2) | collective-permute-done | bytes 524320 | tf_op jit(solution)/shard_map/cond/branch_3_fun/ppermute | solution.py:28
  19.8 0.0 copy-start
  19.8 27.7 %conditional.3 = (bf16[32,16,512]{2,1,0:T(8,128)(2,1)S(1)}) conditional(s32[]{:T(128)} %bitcast.5, bf16[32,16,512]{2,1,0:T(8,128)(2,1)S(1)} %get-tuple-element.47, bf16[32,16,512]{2,1,0:T(8,128)(2,1)S(1)} %get-tuple-element.47, bf16[32,16,512]{2,1,0:T(8,128)(2,1)S(1)} %get-tuple-element.47, ...), branch_computations={%region_4.5_spmd, %region_5.6_spmd, %region_6.7_spmd, %region_7.8_... | conditional | bytes 3145776 | solution.py:50
  19.8 4.3 %collective-permute-start.3 = (bf16[32,16,512]{2,1,0:T(8,128)(2,1)S(1)}, bf16[32,16,512]{2,1,0:T(8,128)(2,1)S(1)}, u32[]{:S(2)}, u32[]{:S(2)}) collective-permute-start(bf16[32,16,512]{2,1,0:T(8,128)(2,1)S(1)} %param.5), channel_id=1, source_target_pairs={{0,32},{8,40},{16,48},{24,56},{32,64},{40,72},{48,80},{56,88},{64,... | collective-permute-start | bytes 1572872 | tf_op jit(solution)/shard_map/cond/branch_1_fun/ppermute | solution.py:28
  24.1 23.3 %collective-permute-done.3 = bf16[32,16,512]{2,1,0:T(8,128)(2,1)S(1)} collective-permute-done((bf16[32,16,512]{2,1,0:T(8,128)(2,1)S(1)}, bf16[32,16,512]{2,1,0:T(8,128)(2,1)S(1)}, u32[]{:S(2)}, u32[]{:S(2)}) %collective-permute-start.3) | collective-permute-done | bytes 524320 | tf_op jit(solution)/shard_map/cond/branch_1_fun/ppermute | solution.py:28
  47.5 0.1 pad_add_fusion.1.places
  47.6 1.2 %multiply_convert_fusion.1 = (bf16[128,512]{1,0:T(8,128)(2,1)S(1)}, bf16[128,512]{1,0:T(8,128)(2,1)S(1)}) fusion(s32[128]{0:T(128)S(1)} %iota_add_fusion), kind=kLoop, calls=%fused_computation.8 | loop fusion | flops 1245184 | bytes 262656 | tf_op jit(solution)/shard_map/convert
  48.8 0.0 collective-permute-done.10.refs_3_
  48.8 0.0 collective-permute-done.11.refs_1_
  48.8 0.0 collective-permute-done.12.refs_2_
  48.8 0.0 collective-permute-done.13.refs_0_
  48.8 0.1 collective-permute-start.14
  48.9 2.7 %collective-permute-start.15 = (bf16[32,16,512]{2,1,0:T(8,128)(2,1)S(1)}, bf16[32,16,512]{2,1,0:T(8,128)(2,1)S(1)}, u32[]{:S(2)}, u32[]{:S(2)}) collective-permute-start(bf16[32,16,512]{2,1,0:T(8,128)(2,1)S(1)} %collective-permute-done.13.refs_0_), channel_id=1, source_target_pairs={{0,6},{1,7},{2,0},{3,1},{4,2},{5,3},{6,4},{7,5},{8,14},{9,15},{10,... | collective-permute-start | bytes 1572872 | tf_op jit(solution)/shard_map/ppermute | solution.py:28
  51.6 0.0 collective-permute-start.16
  51.6 0.1 pad_add_fusion.places
  51.7 0.0 copy-done
  51.7 10.2 %shard_map.37 = (bf16[256,32,128]{2,1,0:T(8,128)(2,1)}, bf16[64,256,128]{2,1,0:T(8,128)(2,1)S(1)}) custom-call(s32[4]{0:T(128)S(1)} %pad_add_fusion.1.places, bf16[32,16,512]{2,1,0:T(8,128)(2,1)S(1)} %bitcast.17, bf16[32,16,512]{2,1,0:T(8,128)(2,1)S(1)} %collective-permute-done.11.refs_1_, bf16[32,16,512]{2,1,0:T(8,128)(2,1)S(1)} %collective-permute-done.12.refs_2_, ...), custom_call_target="tpu_custom_call" | custom-call | flops 3221225472 | bytes 8388608 | tf_op jit(solution)/shard_map/pallas_call | solution.py:155
  61.9 0.9 %collective-permute-done.14.refs_1_ = bf16[32,16,512]{2,1,0:T(8,128)(2,1)S(1)} collective-permute-done((bf16[32,16,512]{2,1,0:T(8,128)(2,1)S(1)}, bf16[32,16,512]{2,1,0:T(8,128)(2,1)S(1)}, u32[]{:S(2)}, u32[]{:S(2)}) %collective-permute-start.14) | collective-permute-done | bytes 524320 | tf_op jit(solution)/shard_map/ppermute | solution.py:28
  62.9 0.0 collective-permute-done.15.refs_2_
  62.9 3.4 %collective-permute-done.16.refs_3_ = bf16[32,16,512]{2,1,0:T(8,128)(2,1)S(1)} collective-permute-done((bf16[32,16,512]{2,1,0:T(8,128)(2,1)S(1)}, bf16[32,16,512]{2,1,0:T(8,128)(2,1)S(1)}, u32[]{:S(2)}, u32[]{:S(2)}) %collective-permute-start.16) | collective-permute-done | bytes 524320 | tf_op jit(solution)/shard_map/ppermute | solution.py:36
  66.3 9.4 %shard_map.38 = bf16[256,32,128]{2,1,0:T(8,128)(2,1)} custom-call(s32[4]{0:T(128)S(1)} %pad_add_fusion.places, bf16[32,16,512]{2,1,0:T(8,128)(2,1)S(1)} %collective-permute-done.13.refs_0_, bf16[32,16,512]{2,1,0:T(8,128)(2,1)S(1)} %collective-permute-done.14.refs_1_, ...), custom_call_target="tpu_custom_call", output_to_operand_aliasing={{}: (7, {})} | custom-call | flops 3221225472 | bytes 8388608 | tf_op jit(solution)/shard_map/pallas_call | solution.py:155
  (4 shorter events, 0.1 us)
Async XLA Ops:
  1.0 47.8 %collective-permute-start.10 = (bf16[32,16,512]{2,1,0:T(8,128)(2,1)}, bf16[32,16,512]{2,1,0:T(8,128)(2,1)S(1)}, u32[]{:S(2)}, u32[]{:S(2)}) collective-permute-start(bf16[32,16,512]{2,1,0:T(8,128)(2,1)} %bitcast.13), channel_id=1, source_target_pairs={{0,4},{1,5},{2,6},{3,7},{4,0},{5,1},{6,2},{7,3},{8,12},{9,13},{10,... | collective-permute-start | bytes 1572872 | tf_op jit(solution)/shard_map/ppermute | solution.py:28
  3.8 45.0 %collective-permute-start.11 = (bf16[32,16,512]{2,1,0:T(8,128)(2,1)}, bf16[32,16,512]{2,1,0:T(8,128)(2,1)S(1)}, u32[]{:S(2)}, u32[]{:S(2)}) collective-permute-start(bf16[32,16,512]{2,1,0:T(8,128)(2,1)} %bitcast.14), channel_id=1, source_target_pairs={{0,2},{1,3},{2,4},{3,5},{4,6},{5,7},{6,0},{7,1},{8,10},{9,11},{10,... | collective-permute-start | bytes 1572872 | tf_op jit(solution)/shard_map/ppermute | solution.py:28
  4.1 44.7 %collective-permute-start.12 = (bf16[32,16,512]{2,1,0:T(8,128)(2,1)}, bf16[32,16,512]{2,1,0:T(8,128)(2,1)S(1)}, u32[]{:S(2)}, u32[]{:S(2)}) collective-permute-start(bf16[32,16,512]{2,1,0:T(8,128)(2,1)} %bitcast.15), channel_id=1, source_target_pairs={{0,6},{1,7},{2,0},{3,1},{4,2},{5,3},{6,4},{7,5},{8,14},{9,15},{10,... | collective-permute-start | bytes 1572872 | tf_op jit(solution)/shard_map/ppermute | solution.py:28
  6.5 42.4 %collective-permute-start.13 = (bf16[32,16,512]{2,1,0:T(8,128)(2,1)}, bf16[32,16,512]{2,1,0:T(8,128)(2,1)S(1)}, u32[]{:S(2)}, u32[]{:S(2)}) collective-permute-start(bf16[32,16,512]{2,1,0:T(8,128)(2,1)} %bitcast.16), channel_id=1, source_target_pairs={{0,1},{1,0},{2,3},{3,2},{4,5},{5,4},{6,7},{7,6},{8,9},{9,8},{10,11... | collective-permute-start | bytes 1572872 | tf_op jit(solution)/shard_map/ppermute | solution.py:36
  9.2 10.6 %collective-permute-start.2 = (bf16[32,16,512]{2,1,0:T(8,128)(2,1)S(1)}, bf16[32,16,512]{2,1,0:T(8,128)(2,1)S(1)}, u32[]{:S(2)}, u32[]{:S(2)}) collective-permute-start(bf16[32,16,512]{2,1,0:T(8,128)(2,1)S(1)} %param.3), channel_id=1, source_target_pairs={{0,248},{8,0},{16,8},{24,16},{32,24},{40,32},{48,40},{56,48},{64,5... | collective-permute-start | bytes 1572872 | tf_op jit(solution)/shard_map/cond/branch_3_fun/ppermute | solution.py:28
  19.8 31.9 %copy-start = (bf16[32,2,8,512]{3,2,1,0:T(8,128)(2,1)S(1)}, bf16[32,2,8,512]{3,2,1,0:T(8,128)(2,1)}, u32[]{:S(2)}) copy-start(bf16[32,2,8,512]{3,2,1,0:T(8,128)(2,1)} %param.15) | copy-start | bytes 1572868
  19.8 27.6 %collective-permute-start.3 = (bf16[32,16,512]{2,1,0:T(8,128)(2,1)S(1)}, bf16[32,16,512]{2,1,0:T(8,128)(2,1)S(1)}, u32[]{:S(2)}, u32[]{:S(2)}) collective-permute-start(bf16[32,16,512]{2,1,0:T(8,128)(2,1)S(1)} %param.5), channel_id=1, source_target_pairs={{0,32},{8,40},{16,48},{24,56},{32,64},{40,72},{48,80},{56,88},{64,... | collective-permute-start | bytes 1572872 | tf_op jit(solution)/shard_map/cond/branch_1_fun/ppermute | solution.py:28
  48.8 14.0 %collective-permute-start.14 = (bf16[32,16,512]{2,1,0:T(8,128)(2,1)S(1)}, bf16[32,16,512]{2,1,0:T(8,128)(2,1)S(1)}, u32[]{:S(2)}, u32[]{:S(2)}) collective-permute-start(bf16[32,16,512]{2,1,0:T(8,128)(2,1)S(1)} %collective-permute-done.13.refs_0_), channel_id=1, source_target_pairs={{0,2},{1,3},{2,4},{3,5},{4,6},{5,7},{6,0},{7,1},{8,10},{9,11},{10,... | collective-permute-start | bytes 1572872 | tf_op jit(solution)/shard_map/ppermute | solution.py:28
  48.9 14.0 %collective-permute-start.15 = (bf16[32,16,512]{2,1,0:T(8,128)(2,1)S(1)}, bf16[32,16,512]{2,1,0:T(8,128)(2,1)S(1)}, u32[]{:S(2)}, u32[]{:S(2)}) collective-permute-start(bf16[32,16,512]{2,1,0:T(8,128)(2,1)S(1)} %collective-permute-done.13.refs_0_), channel_id=1, source_target_pairs={{0,6},{1,7},{2,0},{3,1},{4,2},{5,3},{6,4},{7,5},{8,14},{9,15},{10,... | collective-permute-start | bytes 1572872 | tf_op jit(solution)/shard_map/ppermute | solution.py:28
  51.6 14.7 %collective-permute-start.16 = (bf16[32,16,512]{2,1,0:T(8,128)(2,1)S(1)}, bf16[32,16,512]{2,1,0:T(8,128)(2,1)S(1)}, u32[]{:S(2)}, u32[]{:S(2)}) collective-permute-start(bf16[32,16,512]{2,1,0:T(8,128)(2,1)S(1)} %collective-permute-done.10.refs_3_), channel_id=1, source_target_pairs={{0,1},{1,0},{2,3},{3,2},{4,5},{5,4},{6,7},{7,6},{8,9},{9,8},{10,11... | collective-permute-start | bytes 1572872 | tf_op jit(solution)/shard_map/ppermute | solution.py:36
